TPU v7x, 32 devices: a whole 2x2x4 slice. The times are simulated.
32 devices in a mesh: rep: 8 (over y, x, core), shard: 4 (over z).
Axes of the slice: x: 2, y: 2, z: 4, core: 2. Of those that a mesh axis runs over, the one named last changes fastest.
Arguments:
- grads_matrix: bfloat16 [8, 4, 3, 1024, 1024], P('rep', 'shard'), may hold values from -400 to 400
- grads_vector: bfloat16 [8, 4, 5, 1024], P('rep', 'shard'), may hold values from -6 to 6
- master_matrix: float32 [3, 1024, 1024], P(None, 'shard'), may hold values from -0.1875 to 0.1875
- master_vector: float32 [5, 1024], P(None, 'shard'), may hold values from 0.5 to 1.5
- moment_matrix: float32 [3, 1024, 1024], P(None, 'shard'), may hold values from -4 to 4
- moment_vector: float32 [5, 1024], P(None, 'shard'), may hold values from -4 to 4
- second_matrix: float32 [3, 1024, 1024], P(None, 'shard'), may hold values from 0.05 to 2
- second_vector: float32 [5, 1024], P(None, 'shard'), may hold values from 0.05 to 2
Outputs:
- matrix_master: float32 [3, 1024, 1024], P(None, 'shard')
- vector_master: float32 [5, 1024], P(None, 'shard')
- matrix_moment: float32 [3, 1024, 1024], P(None, 'shard')
- vector_moment: float32 [5, 1024], P(None, 'shard')
- matrix_second: float32 [3, 1024, 1024], P(None, 'shard')
- vector_second: float32 [5, 1024], P(None, 'shard')
- matrix_weights: bfloat16 [3, 1024, 1024], replicated
- vector_weights: bfloat16 [5, 1024], replicated
All inputs are finite; a program needn't handle non-finite values.
Results may differ from a plain program's by a relative error of at most 0.005.
Values may be sent and summed in bfloat16 or wider, within the bound.
A program may use at most 128 MiB of HBM per device.

v0:
```python
import jax
import jax.numpy as jnp
from jax import lax
from jax.sharding import PartitionSpec as P

STEP = 1000
beta_first = 0.9
beta_second = 0.999
learn_rate = 0.01
decay_rate = 0.1
epsilon = 1e-08


def adam_piece(total, master, moment, second, clip, decay):
    scaled = total * clip
    moment_next = beta_first * moment + (1.0 - beta_first) * scaled
    second_next = beta_second * second + (1.0 - beta_second) * scaled * scaled
    corrected = moment_next / (1.0 - beta_first**STEP)
    spread = jnp.sqrt(second_next / (1.0 - beta_second**STEP))
    update = corrected / (spread + epsilon)
    master_next = master - learn_rate * (update + decay * master)
    return (master_next, moment_next, second_next)


def squares_of(first, second):
    return jnp.sum(first * first) + jnp.sum(second * second)


def body(
    grads_matrix,
    grads_vector,
    master_matrix,
    master_vector,
    moment_matrix,
    moment_vector,
    second_matrix,
    second_vector,
):
    local_matrix = grads_matrix[0, 0].astype(jnp.float32)
    local_vector = grads_vector[0, 0].astype(jnp.float32)
    width = local_vector.shape[1]
    count = 3 * width * width + 5 * width
    part_matrix, part_vector = (
        lax.psum_scatter(
            local_matrix.astype(jnp.bfloat16), "shard", scatter_dimension=1, tiled=True
        ).astype(jnp.float32),
        lax.psum_scatter(
            local_vector.astype(jnp.bfloat16), "shard", scatter_dimension=1, tiled=True
        ).astype(jnp.float32),
    )
    mine_matrix, mine_vector = (
        lax.psum(part_matrix.astype(jnp.bfloat16), "rep").astype(jnp.float32),
        lax.psum(part_vector.astype(jnp.bfloat16), "rep").astype(jnp.float32),
    )
    squares = lax.psum(squares_of(mine_matrix, mine_vector), "shard")
    clip = jnp.minimum(1.0, 1.0 / jnp.sqrt(squares / count + 1e-06))
    master_mat, moment_mat, second_mat = adam_piece(
        mine_matrix, master_matrix, moment_matrix, second_matrix, clip, decay_rate
    )
    master_vec, moment_vec, second_vec = adam_piece(
        mine_vector, master_vector, moment_vector, second_vector, clip, 0.0
    )
    weights_mat, weights_vec = (
        lax.all_gather(master_mat.astype(jnp.bfloat16), "shard", axis=1, tiled=True),
        lax.all_gather(master_vec.astype(jnp.bfloat16), "shard", axis=1, tiled=True),
    )
    return (
        master_mat,
        master_vec,
        moment_mat,
        moment_vec,
        second_mat,
        second_vec,
        weights_mat,
        weights_vec,
    )


def solution(mesh):
    return jax.shard_map(
        body,
        mesh=mesh,
        in_specs=(
            P("rep", "shard", None, None, None),
            P("rep", "shard", None, None),
            P(None, "shard", None),
            P(None, "shard"),
            P(None, "shard", None),
            P(None, "shard"),
            P(None, "shard", None),
            P(None, "shard"),
        ),
        out_specs=(
            P(None, "shard", None),
            P(None, "shard"),
            P(None, "shard", None),
            P(None, "shard"),
            P(None, "shard", None),
            P(None, "shard"),
            P(),
            P(),
        ),
        check_vma=False,
    )
```

profile of v0, /device:TPU:0, one launch (start us, length us, event | category | flops | bytes accessed | tf_op | source)
XLA Modules:
  0.0 356.3 jit_solution(2101009983233991101)
XLA Ops:
  7.2 0.0 reduce-scatter.3.cloned.1.call-start
  7.2 0.7 reduce-scatter.3.cloned.1.call-update
  7.9 0.0 copy-start
  7.9 0.0 reduce-scatter.5.cloned.1.call-start
  8.0 0.7 reduce-scatter.5.cloned.1.call-update
  8.7 0.0 all-reduce.2.cloned.1.call-start
  8.7 115.1 %reduce-scatter.3.cloned.1.call-done = bf16[3,256,1024]{2,1,0:T(8,128)(2,1)} async-done(((bf16[3,1024,1024]{2,1,0:T(8,128)(2,1)}), bf16[3,256,1024]{2,1,0:T(8,128)(2,1)}) %reduce-scatter.3.cloned.1.call-update) | async-done | bytes 1572880 | tf_op jit(solution)/shard_map/reduce_scatter | solution.py:44
  123.8 0.0 all-reduce.2.cloned.1.call-update
  123.8 0.0 all-gather.2.cloned.1.call-start
  123.9 21.6 %reduce-scatter.5.cloned.1.call-done = bf16[5,256]{1,0:T(8,128)(2,1)} async-done(((bf16[5,1024]{1,0:T(8,128)(2,1)}), bf16[5,256]{1,0:T(8,128)(2,1)}) %reduce-scatter.5.cloned.1.call-update) | async-done | bytes 2576 | tf_op jit(solution)/shard_map/reduce_scatter | solution.py:47
  145.4 12.0 %psum.22 = bf16[5,256]{1,0:T(8,128)(2,1)S(1)} all-reduce(bf16[5,256]{1,0:T(8,128)(2,1)} %reduce-scatter.5.cloned.1.call-done), channel_id=1, replica_groups=mesh['rep'=8,'shard'=4] {'rep'}, use_global_device_ids=true, to_apply=%region_4.0 | all-reduce | flops 1280 | bytes 5120 | tf_op jit(solution)/shard_map/psum | solution.py:53
  157.5 0.6 fusion.6
  158.1 48.1 %all-reduce.2.cloned.1.call-done = bf16[3,256,1024]{2,1,0:T(8,128)(2,1)} async-done(((bf16[3,256,1024]{2,1,0:T(8,128)(2,1)}), bf16[3,256,1024]{2,1,0:T(8,128)(2,1)}) %all-reduce.2.cloned.1.call-update) | async-done | bytes 1572880 | tf_op jit(solution)/shard_map/psum | solution.py:52
  206.2 2.8 fusion.2
  210.3 12.3 %psum.23 = f32[]{:T(128)} all-reduce(f32[]{:T(128)S(6)} %add.46), channel_id=1, replica_groups=mesh['rep'=8,'shard'=4] {'shard'}, use_global_device_ids=true, to_apply=%region_6.0 | all-reduce | flops 1 | bytes 8 | tf_op jit(solution)/shard_map/psum | solution.py:55
  223.3 0.0 copy-done
  223.4 0.0 copy-start.1
  223.4 0.0 copy-start.2
  223.4 0.0 copy-start.3
  223.4 7.5 %fusion.11 = (bf16[3,256,1024]{2,1,0:T(8,128)(2,1)}, f32[3,256,1024]{2,1,0:T(8,128)}, f32[3,256,1024]{2,1,0:T(8,128)}, f32[3,256,1024]{2,1,0:T(8,128)}) fusion(f32[3,256,1024]{2,1,0:T(8,128)S(1)} %copy-done, f32[]{:T(128)S(6)} %min.3, bf16[3,256,1024]{2,1,0:T(8,128)(2,1)} %all-reduce.2.cloned.1.call-done, f32[3,256,1024]{2,1,0:T(8,128)} %param.14, ...), kind=kLoop, calls=%fused_computation.17 | loop fusion | flops 13369344 | bytes 22020100 | tf_op jit(solution)/shard_map/convert_element_type | solution.py:64
  230.9 0.0 all-gather.2.cloned.1.call-update
  230.9 0.0 copy-done.1
  230.9 0.0 copy-done.2
  230.9 0.0 copy-done.3
  231.0 0.6 fusion.8
  231.6 13.2 %all_gather.7 = bf16[5,1024]{1,0:T(8,128)(2,1)S(1)} all-gather(bf16[5,256]{1,0:T(8,128)(2,1)S(1)} %get-tuple-element.8), channel_id=1, replica_groups=mesh['rep'=8,'shard'=4] {'shard'}, dimensions={1}, use_global_device_ids=true | all-gather | bytes 12800 | tf_op jit(solution)/shard_map/all_gather | solution.py:65
  244.8 98.1 %all-gather.2.cloned.1.call-done = bf16[3,1024,1024]{2,1,0:T(8,128)(2,1)} async-done(((bf16[3,256,1024]{2,1,0:T(8,128)(2,1)}), bf16[3,1024,1024]{2,1,0:T(8,128)(2,1)}) %all-gather.2.cloned.1.call-update) | async-done | bytes 6291472 | tf_op jit(solution)/shard_map/all_gather | solution.py:64
  342.9 6.2 %copy.19 = bf16[3,1024,1024]{2,1,0:T(8,128)(2,1)} copy(bf16[3,1024,1024]{2,1,0:T(8,128)(2,1)} %all-gather.2.cloned.1.call-done) | data formatting | bytes 12582912
  349.1 0.6 copy.20
Async XLA Ops:
  7.2 116.6 %reduce-scatter.3.cloned.1.call-start = ((), (), s32[]{:S(2)}) async-start(), calls=%async_computation.2 | async-start | bytes 7864320 | tf_op jit(solution)/shard_map/reduce_scatter | solution.py:44
  7.9 215.5 %copy-start = (f32[3,256,1024]{2,1,0:T(8,128)S(1)}, f32[3,256,1024]{2,1,0:T(8,128)}, u32[]{:S(2)}) copy-start(f32[3,256,1024]{2,1,0:T(8,128)} %param.10) | copy-start | bytes 9437188
  7.9 137.5 %reduce-scatter.5.cloned.1.call-start = ((), (), s32[]{:S(2)}) async-start(), calls=%async_computation.4 | async-start | bytes 20480 | tf_op jit(solution)/shard_map/reduce_scatter | solution.py:47
  8.7 197.5 %all-reduce.2.cloned.1.call-start = ((), (), s32[]{:S(2)}) async-start(), calls=%async_computation.3 | async-start | bytes 3145728 | tf_op jit(solution)/shard_map/psum | solution.py:52
  123.8 219.1 %all-gather.2.cloned.1.call-start = ((), (), s32[]{:S(2)}) async-start(), calls=%async_computation.5 | async-start | bytes 7864320 | tf_op jit(solution)/shard_map/all_gather | solution.py:64
  223.4 7.6 %copy-start.1 = (f32[5,256]{1,0:T(8,128)S(1)}, f32[5,256]{1,0:T(8,128)}, u32[]{:S(2)}) copy-start(f32[5,256]{1,0:T(8,128)} %param.11) | copy-start | bytes 15364
  223.4 7.6 %copy-start.2 = (f32[5,256]{1,0:T(8,128)S(1)}, f32[5,256]{1,0:T(8,128)}, u32[]{:S(2)}) copy-start(f32[5,256]{1,0:T(8,128)} %param.15) | copy-start | bytes 15364
  223.4 7.6 %copy-start.3 = (f32[5,256]{1,0:T(8,128)S(1)}, f32[5,256]{1,0:T(8,128)}, u32[]{:S(2)}) copy-start(f32[5,256]{1,0:T(8,128)} %param.13) | copy-start | bytes 15364
Sparse Core Ops, SparseCore 0:
  10.3 113.4 reduce-scatter.2
  126.0 19.3 reduce-scatter.4
  149.0 57.1 all-reduce.1
  231.0 111.8 all-gather.1
where the time goes:
time: 357 us; the launch traced here: 356 us
  waiting for transfers between devices  284 us (80%)
  blocking collectives  37.6 us (11%)
  between operations  15.8 us (4%)
  other arithmetic  11.6 us (3%)
  local copies, waits for them, and re-layouts  6.82 us (2%)
    reduce_scatter x1, waiting for transfers between devices, body(): lax.psum_scatter(local_matrix.astype(jnp.bfloat16), 'shard', scatter_dime...  115 us
    all_gather x1, waiting for transfers between devices, body(): lax.all_gather(master_mat.astype(jnp.bfloat16), 'shard', axis=1, tiled=True)  98.1 us
    psum x1, waiting for transfers between devices, body(): lax.psum(part_matrix.astype(jnp.bfloat16), 'rep').astype(jnp.float32)  48.1 us
    reduce_scatter x1, waiting for transfers between devices, body(): lax.psum_scatter(local_vector.astype(jnp.bfloat16), 'shard', scatter_dime...  21.6 us
    all_gather x1, blocking collectives, body(): lax.all_gather(master_vec.astype(jnp.bfloat16), 'shard', axis=1, tiled=True)  13.2 us
    psum x1, blocking collectives, body(): squares = lax.psum(squares_of(mine_matrix, mine_vector), 'shard')  12.3 us
    psum x1, blocking collectives, body(): lax.psum(part_vector.astype(jnp.bfloat16), 'rep').astype(jnp.float32)  12 us
    convert_element_type x1, other arithmetic, body(): master_mat.astype(jnp.bfloat16)  7.51 us
  transfers between devices with their start and end apart: 4, of which 4 were waited for; matrix products, arithmetic and copies ran while one was open for 0% of the time, Pallas kernels for 0%

commit v1 on v0

--- a/solution.py
+++ b/solution.py
@@ -9,6 +9,28 @@
 learn_rate = 0.01
 decay_rate = 0.1
 epsilon = 1e-08
+
+
+def joined_along(blocks, dim):
+    blocks = jnp.moveaxis(blocks, 0, dim)
+    shape = blocks.shape
+    return blocks.reshape(*shape[:dim], shape[dim] * shape[dim + 1], *shape[dim + 2 :])
+
+
+def doubled(x, axis):
+    peers = lax.axis_size(axis)
+    blocks = x[None]
+    for level in range(peers.bit_length() - 1):
+        apart = 1 << level
+        theirs = lax.ppermute(blocks, axis, [(i, i ^ apart) for i in range(peers)])
+        both = jnp.stack([blocks, theirs])
+        upper = lax.axis_index(axis) >> level & 1
+        blocks = jnp.where(upper == 0, both, both[::-1]).reshape(-1, *x.shape)
+    return blocks
+
+
+def collect(array, axis, dim):
+    return joined_along(doubled(array, axis), dim)
 
 
 def adam_piece(total, master, moment, second, clip, decay):
@@ -62,7 +84,7 @@
     )
     weights_mat, weights_vec = (
         lax.all_gather(master_mat.astype(jnp.bfloat16), "shard", axis=1, tiled=True),
-        lax.all_gather(master_vec.astype(jnp.bfloat16), "shard", axis=1, tiled=True),
+        collect(master_vec.astype(jnp.bfloat16), "shard", 1),
     )
     return (
         master_mat,

time: 357 us -> 356 us (level)
  blocking collectives: 37.6 us -> 24.4 us
  waiting for transfers between devices: 284 us -> 297 us
    all_gather x1 -> x0, blocking collectives: 13.2 us -> none  [body(): lax.all_gather(master_vec.astype(jnp.bfloat16), 'shard', axis=1, tiled=True)]
    ppermute x0 -> x2, waiting for transfers between devices: none -> 8.23 us  [doubled(): theirs = lax.ppermute(blocks, axis, [(i, i ^ apart) for i in range(peers)])]
    all_gather x1, waiting for transfers between devices: 98.1 us -> 102 us  [body(): lax.all_gather(master_mat.astype(jnp.bfloat16), 'shard', axis=1, tiled=True)]
  transfers between devices with their start and end apart: 4 -> 6, of which waited for: 4 -> 6; matrix products, arithmetic and copies ran while one was open for 0% -> 1% of each run, Pallas kernels for 0% -> 0%
where the time goes in v1:
time: 356 us
  waiting for transfers between devices  297 us (83%)
  blocking collectives  24.4 us (7%)
  between operations  15.9 us (4%)
  other arithmetic  11.6 us (3%)
  local copies, waits for them, and re-layouts  6.84 us (2%)
    reduce_scatter x1, waiting for transfers between devices, body(): lax.psum_scatter(local_matrix.astype(jnp.bfloat16), 'shard', scatter_dime...  115 us
    all_gather x1, waiting for transfers between devices, body(): lax.all_gather(master_mat.astype(jnp.bfloat16), 'shard', axis=1, tiled=True)  102 us
    psum x1, waiting for transfers between devices, body(): lax.psum(part_matrix.astype(jnp.bfloat16), 'rep').astype(jnp.float32)  48.1 us
    reduce_scatter x1, waiting for transfers between devices, body(): lax.psum_scatter(local_vector.astype(jnp.bfloat16), 'shard', scatter_dime...  21.6 us
    psum x1, blocking collectives, body(): squares = lax.psum(squares_of(mine_matrix, mine_vector), 'shard')  12.3 us
    psum x1, blocking collectives, body(): lax.psum(part_vector.astype(jnp.bfloat16), 'rep').astype(jnp.float32)  12 us
    ppermute x2, waiting for transfers between devices, doubled(): theirs = lax.ppermute(blocks, axis, [(i, i ^ apart) for i in range(peers)])  8.23 us
    convert_element_type x1, other arithmetic, body(): master_mat.astype(jnp.bfloat16)  7.51 us
  transfers between devices with their start and end apart: 6, of which 6 were waited for; matrix products, arithmetic and copies ran while one was open for 1% of the time, Pallas kernels for 0%

profile of v1, /device:TPU:0, one launch (start us, length us, event | category | flops | bytes accessed | tf_op | source)
XLA Modules:
  0.0 355.6 jit_solution(15740956770587087819)
XLA Ops:
  7.2 0.0 reduce-scatter.3.cloned.1.call-start
  7.2 0.7 reduce-scatter.3.cloned.1.call-update
  7.9 0.0 copy-start
  7.9 0.0 reduce-scatter.5.cloned.1.call-start
  8.0 0.7 reduce-scatter.5.cloned.1.call-update
  8.7 0.0 all-reduce.2.cloned.1.call-start
  8.7 115.1 %reduce-scatter.3.cloned.1.call-done = bf16[3,256,1024]{2,1,0:T(8,128)(2,1)} async-done(((bf16[3,1024,1024]{2,1,0:T(8,128)(2,1)}), bf16[3,256,1024]{2,1,0:T(8,128)(2,1)}) %reduce-scatter.3.cloned.1.call-update) | async-done | bytes 1572880 | tf_op jit(solution)/shard_map/reduce_scatter | solution.py:66
  123.8 0.0 all-reduce.2.cloned.1.call-update
  123.8 0.0 all-gather.2.cloned.1.call-start
  123.9 21.6 %reduce-scatter.5.cloned.1.call-done = bf16[5,256]{1,0:T(8,128)(2,1)} async-done(((bf16[5,1024]{1,0:T(8,128)(2,1)}), bf16[5,256]{1,0:T(8,128)(2,1)}) %reduce-scatter.5.cloned.1.call-update) | async-done | bytes 2576 | tf_op jit(solution)/shard_map/reduce_scatter | solution.py:69
  145.4 12.0 %psum.22 = bf16[5,256]{1,0:T(8,128)(2,1)S(1)} all-reduce(bf16[5,256]{1,0:T(8,128)(2,1)} %reduce-scatter.5.cloned.1.call-done), channel_id=1, replica_groups=mesh['rep'=8,'shard'=4] {'rep'}, use_global_device_ids=true, to_apply=%region_4.0 | all-reduce | flops 1280 | bytes 5120 | tf_op jit(solution)/shard_map/psum | solution.py:75
  157.5 0.6 fusion.6
  158.1 48.1 %all-reduce.2.cloned.1.call-done = bf16[3,256,1024]{2,1,0:T(8,128)(2,1)} async-done(((bf16[3,256,1024]{2,1,0:T(8,128)(2,1)}), bf16[3,256,1024]{2,1,0:T(8,128)(2,1)}) %all-reduce.2.cloned.1.call-update) | async-done | bytes 1572880 | tf_op jit(solution)/shard_map/psum | solution.py:74
  206.2 2.8 fusion.2
  210.3 12.3 %psum.23 = f32[]{:T(128)} all-reduce(f32[]{:T(128)S(6)} %add.46), channel_id=1, replica_groups=mesh['rep'=8,'shard'=4] {'shard'}, use_global_device_ids=true, to_apply=%region_6.0 | all-reduce | flops 1 | bytes 8 | tf_op jit(solution)/shard_map/psum | solution.py:77
  223.3 0.0 copy-done
  223.4 0.0 copy-start.2
  223.4 0.0 copy-start.3
  223.4 0.0 copy-start.4
  223.4 7.5 %fusion.12 = (bf16[3,256,1024]{2,1,0:T(8,128)(2,1)}, f32[3,256,1024]{2,1,0:T(8,128)}, f32[3,256,1024]{2,1,0:T(8,128)}, f32[3,256,1024]{2,1,0:T(8,128)}) fusion(f32[3,256,1024]{2,1,0:T(8,128)S(1)} %copy-done, f32[]{:T(128)S(6)} %min.3, bf16[3,256,1024]{2,1,0:T(8,128)(2,1)} %all-reduce.2.cloned.1.call-done, f32[3,256,1024]{2,1,0:T(8,128)} %param.14, ...), kind=kLoop, calls=%fused_computation.25 | loop fusion | flops 13369344 | bytes 22020100 | tf_op jit(solution)/shard_map/convert_element_type | solution.py:86
  230.9 0.0 all-gather.2.cloned.1.call-update
  230.9 0.0 copy-done.2
  230.9 0.0 copy-done.3
  231.0 0.6 convert_bitcast_fusion.1
  231.6 0.0 collective-permute-start
  231.6 3.6 %collective-permute-done = bf16[1,5,256]{2,1,0:T(8,128)(2,1)S(1)} collective-permute-done((bf16[1,5,256]{2,1,0:T(8,128)(2,1)S(1)}, bf16[1,5,256]{2,1,0:T(8,128)(2,1)S(1)}, u32[]{:S(2)}, u32[]{:S(2)}) %collective-permute-start) | collective-permute-done | bytes 2592 | tf_op jit(solution)/shard_map/ppermute | solution.py:25
  235.2 0.1 collective-permute-start.1
  235.3 4.6 %collective-permute-done.1 = bf16[2,5,256]{2,1,0:T(8,128)(2,1)S(1)} collective-permute-done((bf16[2,5,256]{2,1,0:T(8,128)(2,1)S(1)}, bf16[2,5,256]{2,1,0:T(8,128)(2,1)S(1)}, u32[]{:S(2)}, u32[]{:S(2)}) %collective-permute-start.1) | collective-permute-done | bytes 5152 | tf_op jit(solution)/shard_map/ppermute | solution.py:25
  240.0 0.6 copy.17
  240.6 102.3 %all-gather.2.cloned.1.call-done = bf16[3,1024,1024]{2,1,0:T(8,128)(2,1)} async-done(((bf16[3,256,1024]{2,1,0:T(8,128)(2,1)}), bf16[3,1024,1024]{2,1,0:T(8,128)(2,1)}) %all-gather.2.cloned.1.call-update) | async-done | bytes 6291472 | tf_op jit(solution)/shard_map/all_gather | solution.py:86
  342.9 6.2 %copy.22 = bf16[3,1024,1024]{2,1,0:T(8,128)(2,1)} copy(bf16[3,1024,1024]{2,1,0:T(8,128)(2,1)} %all-gather.2.cloned.1.call-done) | data formatting | bytes 12582912
  349.1 0.0 copy-done.1
  (8 shorter events, 0.0 us)
Async XLA Ops:
  7.2 116.6 %reduce-scatter.3.cloned.1.call-start = ((), (), s32[]{:S(2)}) async-start(), calls=%async_computation.2 | async-start | bytes 7864320 | tf_op jit(solution)/shard_map/reduce_scatter | solution.py:66
  7.9 215.5 %copy-start = (f32[3,256,1024]{2,1,0:T(8,128)S(1)}, f32[3,256,1024]{2,1,0:T(8,128)}, u32[]{:S(2)}) copy-start(f32[3,256,1024]{2,1,0:T(8,128)} %param.10) | copy-start | bytes 9437188
  7.9 137.5 %reduce-scatter.5.cloned.1.call-start = ((), (), s32[]{:S(2)}) async-start(), calls=%async_computation.4 | async-start | bytes 20480 | tf_op jit(solution)/shard_map/reduce_scatter | solution.py:69
  8.7 197.5 %all-reduce.2.cloned.1.call-start = ((), (), s32[]{:S(2)}) async-start(), calls=%async_computation.3 | async-start | bytes 3145728 | tf_op jit(solution)/shard_map/psum | solution.py:74
  123.8 219.1 %all-gather.2.cloned.1.call-start = ((), (), s32[]{:S(2)}) async-start(), calls=%async_computation.5 | async-start | bytes 7864320 | tf_op jit(solution)/shard_map/all_gather | solution.py:86
  223.4 7.6 %copy-start.2 = (f32[5,256]{1,0:T(8,128)S(1)}, f32[5,256]{1,0:T(8,128)}, u32[]{:S(2)}) copy-start(f32[5,256]{1,0:T(8,128)} %param.11) | copy-start | bytes 15364
  223.4 7.6 %copy-start.3 = (f32[5,256]{1,0:T(8,128)S(1)}, f32[5,256]{1,0:T(8,128)}, u32[]{:S(2)}) copy-start(f32[5,256]{1,0:T(8,128)} %param.15) | copy-start | bytes 15364
  223.4 7.6 %copy-start.4 = (f32[5,256]{1,0:T(8,128)S(1)}, f32[5,256]{1,0:T(8,128)}, u32[]{:S(2)}) copy-start(f32[5,256]{1,0:T(8,128)} %param.13) | copy-start | bytes 15364
  231.6 117.5 %copy-start.1 = (f32[5,256]{1,0:T(8,128)}, f32[5,256]{1,0:T(8,128)S(1)}, u32[]{:S(2)}) copy-start(f32[5,256]{1,0:T(8,128)S(1)} %get-tuple-element.27) | copy-start | bytes 15364
  231.6 3.6 %collective-permute-start = (bf16[1,5,256]{2,1,0:T(8,128)(2,1)S(1)}, bf16[1,5,256]{2,1,0:T(8,128)(2,1)S(1)}, u32[]{:S(2)}, u32[]{:S(2)}) collective-permute-start(bf16[1,5,256]{2,1,0:T(8,128)(2,1)S(1)} %convert_bitcast_fusion), channel_id=1, source_target_pairs={{0,1},{1,0},{2,3},{3,2},{4,5},{5,4},{6,7},{7,6},{8,9},{9,8},{10,11... | collective-permute-start | bytes 7688 | tf_op jit(solution)/shard_map/ppermute | solution.py:25
  235.2 4.7 %collective-permute-start.1 = (bf16[2,5,256]{2,1,0:T(8,128)(2,1)S(1)}, bf16[2,5,256]{2,1,0:T(8,128)(2,1)S(1)}, u32[]{:S(2)}, u32[]{:S(2)}) collective-permute-start(bf16[2,5,256]{2,1,0:T(8,128)(2,1)S(1)} %get-tuple-element.17), channel_id=1, source_target_pairs={{0,2},{1,3},{2,0},{3,1},{4,6},{5,7},{6,4},{7,5},{8,10},{9,11},{10,... | collective-permute-start | bytes 15368 | tf_op jit(solution)/shard_map/ppermute | solution.py:25
Sparse Core Ops, SparseCore 0:
  10.3 113.4 reduce-scatter.2
  126.0 19.3 reduce-scatter.4
  149.0 57.1 all-reduce.1
  231.0 111.7 all-gather.1
